TPU v7x, 32 devices: a whole 2x2x4 slice. The times are simulated.
32 devices in a mesh: section: 4 (over z), dp: 4 (over y, x), tensor: 2 (over core).
Axes of the slice: x: 2, y: 2, z: 4, core: 2. Of those that a mesh axis runs over, the one named last changes fastest.
Arguments:
- inputs: bfloat16 [2, 512, 768], P(None, 'dp'), may hold values from -6 to 6
- out_grads: bfloat16 [2, 512, 768], P(None, 'dp'), may hold values from -6 to 6
- norm_gain: float32 [4, 768], P('section'), may hold values from 0.1 to 1.9
- up_weight: bfloat16 [4, 768, 3072], P('section', None, 'tensor'), may hold values from -0.21875 to 0.21875
- down_weight: bfloat16 [4, 3072, 768], P('section', 'tensor'), may hold values from -0.109375 to 0.109375
- prior_up_grad: bfloat16 [4, 4, 768, 3072], P('dp', 'section', None, 'tensor'), may hold values from -6 to 6
- prior_down_grad: bfloat16 [4, 4, 3072, 768], P('dp', 'section', 'tensor'), may hold values from -6 to 6
- master_up: float32 [4, 768, 3072], P('section', 'dp', 'tensor'), may hold values from -0.3 to 0.3
- master_down: float32 [4, 3072, 768], P('section', ('tensor', 'dp')), may hold values from -0.3 to 0.3
Outputs:
- layer_outputs: bfloat16 [4, 2, 512, 768], P('section', None, 'dp')
- input_grads: bfloat16 [4, 2, 512, 768], P('section', None, 'dp')
- new_up: float32 [4, 768, 3072], P('section', 'dp', 'tensor')
- new_down: float32 [4, 3072, 768], P('section', ('tensor', 'dp'))
All inputs are finite; a program needn't handle non-finite values.
Results may differ from a plain program's by a relative error of at most 0.019.
Values may be sent and summed in bfloat16 or wider, within the bound.
A program may use at most 128 MiB of HBM per device.

v0:
```python
import jax
import jax.numpy as jnp
from jax import lax
from jax.sharding import PartitionSpec as P

eps_norm = 1e-05
gelu_coef = 0.7978845608028654
learning_rate = 0.05


def shifted(value, axis, steps):
    count = lax.axis_size(axis)
    initial, last = (max(0, -steps), min(count, count - steps))
    return lax.ppermute(value, axis, [(source, source + steps) for source in range(initial, last)])


def gelu_tanh(value):
    inner = jnp.tanh(gelu_coef * (value + 0.044715 * value * value * value))
    return 0.5 * value * (1.0 + inner)


def gelu_slope(value):
    inner = jnp.tanh(gelu_coef * (value + 0.044715 * value * value * value))
    return 0.5 * (1.0 + inner) + 0.5 * value * (1.0 - inner * inner) * gelu_coef * (
        1.0 + 3.0 * 0.044715 * value * value
    )


def apply_norm(layer_entry_input, gain_vector):
    values = layer_entry_input.astype(jnp.float32)
    center = jnp.mean(values, axis=-1, keepdims=True)
    centered_rows = values - center
    spread = jnp.mean(centered_rows * centered_rows, axis=-1, keepdims=True)
    inverse_scale = lax.rsqrt(spread + eps_norm)
    standardized_input = centered_rows * inverse_scale
    return (
        (standardized_input * gain_vector).astype(jnp.bfloat16),
        standardized_input,
        inverse_scale,
    )


def layer_forward(layer_entry_input, gain_vector, w_up, w_down):
    normalized_rows, standardized_input, inverse_scale = apply_norm(layer_entry_input, gain_vector)
    upper = jnp.dot(normalized_rows, w_up, preferred_element_type=jnp.float32)
    active = gelu_tanh(upper).astype(jnp.bfloat16)
    partial_value = jnp.dot(active, w_down, preferred_element_type=jnp.float32)
    share = lax.psum_scatter(
        partial_value.astype(jnp.bfloat16), "tensor", scatter_dimension=0, tiled=True
    ).astype(jnp.float32)
    half_rows = share.shape[0]
    row_start = lax.axis_index("tensor") * half_rows
    own_rows = lax.dynamic_slice_in_dim(layer_entry_input, row_start, half_rows, 0)
    half_out = (own_rows.astype(jnp.float32) + share).astype(jnp.bfloat16)
    return lax.all_gather(half_out, "tensor", axis=0, tiled=True)


def norm_gradient_pass(
    normalized_gradient, upstream_gradient, gain_vector, standardized_input, inverse_scale
):
    rescaled_rows = normalized_gradient * gain_vector
    leading_operand = jnp.mean(rescaled_rows, axis=-1, keepdims=True)
    trailing_operand = jnp.mean(rescaled_rows * standardized_input, axis=-1, keepdims=True)
    final_output = upstream_gradient.astype(jnp.float32) + inverse_scale * (
        rescaled_rows - leading_operand - standardized_input * trailing_operand
    )
    return final_output.astype(jnp.bfloat16)


def layer_backward(layer_entry_input, upstream_gradient, gain_vector, w_up, w_down):
    normalized_rows, standardized_input, inverse_scale = apply_norm(layer_entry_input, gain_vector)
    upper = jnp.dot(normalized_rows, w_up, preferred_element_type=jnp.float32)
    grad_act = lax.dot_general(
        upstream_gradient, w_down, (((1,), (1,)), ((), ())), preferred_element_type=jnp.float32
    )
    grad_up = (grad_act * gelu_slope(upper)).astype(jnp.bfloat16)
    partial_value = lax.dot_general(
        grad_up, w_up, (((1,), (1,)), ((), ())), preferred_element_type=jnp.float32
    )
    normalized_gradient = lax.psum(partial_value.astype(jnp.bfloat16), "tensor").astype(jnp.float32)
    return norm_gradient_pass(
        normalized_gradient, upstream_gradient, gain_vector, standardized_input, inverse_scale
    )


def store_row(buffer, row_value, slot_index, in_range):
    previous = lax.dynamic_index_in_dim(buffer, slot_index, 0, keepdims=False)
    chosen = jnp.where(in_range, row_value, previous)
    return lax.dynamic_update_index_in_dim(buffer, chosen, slot_index, 0)


def local(
    inputs,
    out_grads,
    norm_gain,
    up_weight,
    down_weight,
    prior_up_grad,
    prior_down_grad,
    master_up,
    master_down,
):
    totals = (
        lax.psum_scatter(
            prior_up_grad.astype(jnp.float32).astype(jnp.bfloat16),
            "dp",
            scatter_dimension=2,
            tiled=True,
        ).astype(jnp.float32),
        lax.psum_scatter(
            prior_down_grad.astype(jnp.float32).astype(jnp.bfloat16),
            "dp",
            scatter_dimension=2,
            tiled=True,
        ).astype(jnp.float32),
    )
    up_total = totals[0][0]
    down_total = totals[1][0]
    new_up = master_up - learning_rate * up_total
    new_down = master_down - learning_rate * down_total
    sections = lax.axis_size("section")
    section_index = lax.axis_index("section")
    micro_count = inputs.shape[0]
    tick_count = micro_count + sections - 1
    gain_vector = norm_gain[0]
    w_up = up_weight[0]
    w_down = down_weight[0]
    stashed = jnp.zeros_like(inputs)
    produced = jnp.zeros_like(inputs)
    carried = jnp.zeros(inputs.shape[1:], jnp.bfloat16)
    for tick in range(tick_count):
        fresh_rows = inputs[min(tick, micro_count - 1)]
        layer_entry_input = jnp.where(section_index == 0, fresh_rows, carried)
        layer_out = layer_forward(layer_entry_input, gain_vector, w_up, w_down)
        micro_index = tick - section_index
        in_range = (micro_index >= 0) & (micro_index < micro_count)
        slot_index = jnp.clip(micro_index, 0, micro_count - 1)
        stashed = store_row(stashed, layer_entry_input, slot_index, in_range)
        produced = store_row(produced, layer_out, slot_index, in_range)
        if tick + 1 < tick_count:
            carried = shifted(layer_out, "section", 1)
    grads_done = jnp.zeros_like(inputs)
    carried_grad = jnp.zeros(inputs.shape[1:], jnp.bfloat16)
    for tick in range(tick_count):
        seed_grad = out_grads[min(tick, micro_count - 1)]
        upstream_gradient = jnp.where(section_index == sections - 1, seed_grad, carried_grad)
        micro_index = tick - (sections - 1 - section_index)
        in_range = (micro_index >= 0) & (micro_index < micro_count)
        slot_index = jnp.clip(micro_index, 0, micro_count - 1)
        layer_entry_input = lax.dynamic_index_in_dim(stashed, slot_index, 0, keepdims=False)
        input_grad = layer_backward(layer_entry_input, upstream_gradient, gain_vector, w_up, w_down)
        grads_done = store_row(grads_done, input_grad, slot_index, in_range)
        if tick + 1 < tick_count:
            carried_grad = shifted(input_grad, "section", -1)
    return (produced[None], grads_done[None], new_up, new_down)


def solution(mesh):
    placed = (
        P(None, "dp", None),
        P(None, "dp", None),
        P("section", None),
        P("section", None, "tensor"),
        P("section", "tensor", None),
        P("dp", "section", None, "tensor"),
        P("dp", "section", "tensor", None),
        P("section", "dp", "tensor"),
        P("section", ("tensor", "dp"), None),
    )
    return jax.shard_map(
        local,
        mesh=mesh,
        in_specs=placed,
        out_specs=(
            P("section", None, "dp", None),
            P("section", None, "dp", None),
            P("section", "dp", "tensor"),
            P("section", ("tensor", "dp"), None),
        ),
        check_vma=False,
    )
```

profile of v0, /device:TPU:0, one launch (start us, length us, event | category | flops | bytes accessed | tf_op | source)
XLA Modules:
  0.0 369.6 jit_solution(16224461375717277040)
XLA Ops:
  7.3 1.1 select_dynamic-update-slice_fusion
  9.5 3.4 fusion.85
  12.9 10.4 %reduce-scatter.8.cloned.1.call-done = bf16[64,768]{1,0:T(8,128)(2,1)} async-done(((bf16[128,768]{1,0:T(8,128)(2,1)}), bf16[64,768]{1,0:T(8,128)(2,1)}) %reduce-scatter.8.cloned.1.call-update) | async-done | bytes 98320 | tf_op jit(solution)/shard_map/reduce_scatter | solution.py:48
  24.2 1.9 all_gather.15
  26.2 4.3 %collective-permute-start = (bf16[128,768]{1,0:T(8,128)(2,1)S(1)}, bf16[128,768]{1,0:T(8,128)(2,1)}, u32[]{:S(2)}, u32[]{:S(2)}) collective-permute-start(bf16[128,768]{1,0:T(8,128)(2,1)S(1)} %all_gather.15), channel_id=1, source_target_pairs={{0,8},{8,16},{16,24},{1,9},{9,17},{17,25},{2,10},{10,18},{18,26},{... | collective-permute-start | bytes 589832 | tf_op jit(solution)/shard_map/ppermute | solution.py:14
  30.5 3.9 %collective-permute-done = bf16[128,768]{1,0:T(8,128)(2,1)} collective-permute-done((bf16[128,768]{1,0:T(8,128)(2,1)S(1)}, bf16[128,768]{1,0:T(8,128)(2,1)}, u32[]{:S(2)}, u32[]{:S(2)}) %collective-permute-start) | collective-permute-done | bytes 196640 | tf_op jit(solution)/shard_map/ppermute | solution.py:14
  34.9 3.3 fusion.88
  38.3 10.6 %reduce-scatter.10.cloned.1.call-done = bf16[64,768]{1,0:T(8,128)(2,1)} async-done(((bf16[128,768]{1,0:T(8,128)(2,1)}), bf16[64,768]{1,0:T(8,128)(2,1)}) %reduce-scatter.10.cloned.1.call-update) | async-done | bytes 98320 | tf_op jit(solution)/shard_map/reduce_scatter | solution.py:48
  49.8 1.9 all_gather.16
  51.8 4.3 %collective-permute-start.1 = (bf16[128,768]{1,0:T(8,128)(2,1)S(1)}, bf16[128,768]{1,0:T(8,128)(2,1)}, u32[]{:S(2)}, u32[]{:S(2)}) collective-permute-start(bf16[128,768]{1,0:T(8,128)(2,1)S(1)} %all_gather.16), channel_id=1, source_target_pairs={{0,8},{8,16},{16,24},{1,9},{9,17},{17,25},{2,10},{10,18},{18,26},{... | collective-permute-start | bytes 589832 | tf_op jit(solution)/shard_map/ppermute | solution.py:14
  56.1 3.9 %collective-permute-done.1 = bf16[128,768]{1,0:T(8,128)(2,1)} collective-permute-done((bf16[128,768]{1,0:T(8,128)(2,1)S(1)}, bf16[128,768]{1,0:T(8,128)(2,1)}, u32[]{:S(2)}, u32[]{:S(2)}) %collective-permute-start.1) | collective-permute-done | bytes 196640 | tf_op jit(solution)/shard_map/ppermute | solution.py:14
  60.4 3.3 fusion.91
  63.8 10.6 %reduce-scatter.12.cloned.1.call-done = bf16[64,768]{1,0:T(8,128)(2,1)} async-done(((bf16[128,768]{1,0:T(8,128)(2,1)}), bf16[64,768]{1,0:T(8,128)(2,1)}) %reduce-scatter.12.cloned.1.call-update) | async-done | bytes 98320 | tf_op jit(solution)/shard_map/reduce_scatter | solution.py:48
  75.4 1.9 all_gather.17
  77.3 4.3 %collective-permute-start.2 = (bf16[128,768]{1,0:T(8,128)(2,1)S(1)}, bf16[128,768]{1,0:T(8,128)(2,1)}, u32[]{:S(2)}, u32[]{:S(2)}) collective-permute-start(bf16[128,768]{1,0:T(8,128)(2,1)S(1)} %all_gather.17), channel_id=1, source_target_pairs={{0,8},{8,16},{16,24},{1,9},{9,17},{17,25},{2,10},{10,18},{18,26},{... | collective-permute-start | bytes 589832 | tf_op jit(solution)/shard_map/ppermute | solution.py:14
  81.6 3.9 %collective-permute-done.2 = bf16[128,768]{1,0:T(8,128)(2,1)} collective-permute-done((bf16[128,768]{1,0:T(8,128)(2,1)S(1)}, bf16[128,768]{1,0:T(8,128)(2,1)}, u32[]{:S(2)}, u32[]{:S(2)}) %collective-permute-start.2) | collective-permute-done | bytes 196640 | tf_op jit(solution)/shard_map/ppermute | solution.py:14
  86.0 3.3 fusion.94
  89.4 10.6 %reduce-scatter.14.cloned.1.call-done = bf16[64,768]{1,0:T(8,128)(2,1)} async-done(((bf16[128,768]{1,0:T(8,128)(2,1)}), bf16[64,768]{1,0:T(8,128)(2,1)}) %reduce-scatter.14.cloned.1.call-update) | async-done | bytes 98320 | tf_op jit(solution)/shard_map/reduce_scatter | solution.py:48
  100.9 1.9 all_gather.18
  102.9 4.3 %collective-permute-start.3 = (bf16[128,768]{1,0:T(8,128)(2,1)S(1)}, bf16[128,768]{1,0:T(8,128)(2,1)}, u32[]{:S(2)}, u32[]{:S(2)}) collective-permute-start(bf16[128,768]{1,0:T(8,128)(2,1)S(1)} %all_gather.18), channel_id=1, source_target_pairs={{0,8},{8,16},{16,24},{1,9},{9,17},{17,25},{2,10},{10,18},{18,26},{... | collective-permute-start | bytes 589832 | tf_op jit(solution)/shard_map/ppermute | solution.py:14
  107.2 3.9 %collective-permute-done.3 = bf16[128,768]{1,0:T(8,128)(2,1)} collective-permute-done((bf16[128,768]{1,0:T(8,128)(2,1)S(1)}, bf16[128,768]{1,0:T(8,128)(2,1)}, u32[]{:S(2)}, u32[]{:S(2)}) %collective-permute-start.3) | collective-permute-done | bytes 196640 | tf_op jit(solution)/shard_map/ppermute | solution.py:14
  113.2 1.4 fusion.38
  114.6 4.2 %fusion.60 = bf16[128,768]{1,0:T(8,128)(2,1)} fusion(bf16[1,768,1536]{2,1,0:T(8,128)(2,1)S(1)} %copy-done, bf16[1,1536,768]{2,1,0:T(8,128)(2,1)} %param.13, f32[128,1536]{1,0:T(8,128)} %fusion.38, bf16[2,128,768]{2,1,0:T(8,128)(2,1)S(1)} %copy-done.2, pred[]{:T(512)S(6)} %eq.5), kind=kOutput, calls=%fused_computation.72 | convolution fusion | flops 607911936 | bytes 5898241 | tf_op jit(solution)/shard_map/dot_general | solution.py:77
  118.9 21.1 %all-reduce.6.cloned.1.call-done = bf16[128,768]{1,0:T(8,128)(2,1)} async-done(((bf16[128,768]{1,0:T(8,128)(2,1)}), bf16[128,768]{1,0:T(8,128)(2,1)}) %all-reduce.6.cloned.1.call-update) | async-done | bytes 196624 | tf_op jit(solution)/shard_map/psum | solution.py:80
  140.0 1.9 fusion.307
  142.0 1.2 bitcast_dynamic-update-slice_fusion.4
  143.2 1.3 collective-permute-start.4
  144.5 2.0 fusion.34
  147.2 5.1 %collective-permute-done.4 = bf16[128,768]{1,0:T(8,128)(2,1)} collective-permute-done((bf16[128,768]{1,0:T(8,128)(2,1)S(1)}, bf16[128,768]{1,0:T(8,128)(2,1)}, u32[]{:S(2)}, u32[]{:S(2)}) %collective-permute-start.4) | collective-permute-done | bytes 196640 | tf_op jit(solution)/shard_map/ppermute | solution.py:14
  152.3 4.2 %fusion.65 = bf16[128,768]{1,0:T(8,128)(2,1)} fusion(bf16[1,768,1536]{2,1,0:T(8,128)(2,1)S(1)} %copy-done, bf16[1,1536,768]{2,1,0:T(8,128)(2,1)} %param.13, f32[128,1536]{1,0:T(8,128)} %fusion.34, bf16[128,768]{1,0:T(8,128)(2,1)} %collective-permute-done.4, pred[]{:T(512)S(6)} %eq.5, bf16[2,128,768]{2,1,0:T(8,128)(2,1)S(1)} %copy-done.2), kind=kOutput, calls=%fused_computation.73 | convolution fusion | flops 607911936 | bytes 6094849 | tf_op jit(solution)/shard_map/dot_general | solution.py:77
  156.6 1.2 add_rsqrt_fusion.2
  157.8 17.2 %all-reduce.8.cloned.1.call-done = bf16[128,768]{1,0:T(8,128)(2,1)} async-done(((bf16[128,768]{1,0:T(8,128)(2,1)}), bf16[128,768]{1,0:T(8,128)(2,1)}) %all-reduce.8.cloned.1.call-update) | async-done | bytes 196624 | tf_op jit(solution)/shard_map/psum | solution.py:80
  175.0 1.1 fusion.314
  176.2 1.4 bitcast_dynamic-update-slice_fusion.3
  177.6 1.5 collective-permute-start.5
  179.0 2.1 fusion.30
  181.1 5.6 %collective-permute-done.5 = bf16[128,768]{1,0:T(8,128)(2,1)} collective-permute-done((bf16[128,768]{1,0:T(8,128)(2,1)S(1)}, bf16[128,768]{1,0:T(8,128)(2,1)}, u32[]{:S(2)}, u32[]{:S(2)}) %collective-permute-start.5) | collective-permute-done | bytes 196640 | tf_op jit(solution)/shard_map/ppermute | solution.py:14
  186.7 4.2 %fusion.70 = bf16[128,768]{1,0:T(8,128)(2,1)} fusion(bf16[1,768,1536]{2,1,0:T(8,128)(2,1)S(1)} %copy-done, bf16[1,1536,768]{2,1,0:T(8,128)(2,1)} %param.13, f32[128,1536]{1,0:T(8,128)} %fusion.30, bf16[128,768]{1,0:T(8,128)(2,1)} %collective-permute-done.5, pred[]{:T(512)S(6)} %eq.5, bf16[2,128,768]{2,1,0:T(8,128)(2,1)S(1)} %copy-done.2), kind=kOutput, calls=%fused_computation.74 | convolution fusion | flops 607911936 | bytes 6094849 | tf_op jit(solution)/shard_map/dot_general | solution.py:77
  191.0 1.2 add_rsqrt_fusion.1
  192.9 16.5 %all-reduce.10.cloned.1.call-done = bf16[128,768]{1,0:T(8,128)(2,1)} async-done(((bf16[128,768]{1,0:T(8,128)(2,1)}), bf16[128,768]{1,0:T(8,128)(2,1)}) %all-reduce.10.cloned.1.call-update) | async-done | bytes 196624 | tf_op jit(solution)/shard_map/psum | solution.py:80
  209.4 1.1 fusion.313
  210.6 1.4 bitcast_dynamic-update-slice_fusion.2
  212.0 1.3 collective-permute-start.6
  213.3 2.0 fusion.26
  215.3 5.8 %collective-permute-done.6 = bf16[128,768]{1,0:T(8,128)(2,1)} collective-permute-done((bf16[128,768]{1,0:T(8,128)(2,1)S(1)}, bf16[128,768]{1,0:T(8,128)(2,1)}, u32[]{:S(2)}, u32[]{:S(2)}) %collective-permute-start.6) | collective-permute-done | bytes 196640 | tf_op jit(solution)/shard_map/ppermute | solution.py:14
  221.1 4.2 %fusion.75 = bf16[128,768]{1,0:T(8,128)(2,1)} fusion(bf16[1,768,1536]{2,1,0:T(8,128)(2,1)S(1)} %copy-done, bf16[1,1536,768]{2,1,0:T(8,128)(2,1)} %param.13, f32[128,1536]{1,0:T(8,128)} %fusion.26, bf16[128,768]{1,0:T(8,128)(2,1)} %collective-permute-done.6, pred[]{:T(512)S(6)} %eq.5, bf16[2,128,768]{2,1,0:T(8,128)(2,1)S(1)} %copy-done.2), kind=kOutput, calls=%fused_computation.75 | convolution fusion | flops 607911936 | bytes 6094849 | tf_op jit(solution)/shard_map/dot_general | solution.py:77
  225.4 3.4 fusion.97
  230.2 13.6 %all-reduce.12.cloned.1.call-done = bf16[128,768]{1,0:T(8,128)(2,1)} async-done(((bf16[128,768]{1,0:T(8,128)(2,1)}), bf16[128,768]{1,0:T(8,128)(2,1)}) %all-reduce.12.cloned.1.call-update) | async-done | bytes 196624 | tf_op jit(solution)/shard_map/psum | solution.py:80
  243.8 1.1 fusion.312
  245.0 1.4 bitcast_dynamic-update-slice_fusion.1
  246.4 1.3 collective-permute-start.7
  247.7 1.4 fusion.22
  249.1 6.4 %collective-permute-done.7 = bf16[128,768]{1,0:T(8,128)(2,1)} collective-permute-done((bf16[128,768]{1,0:T(8,128)(2,1)S(1)}, bf16[128,768]{1,0:T(8,128)(2,1)}, u32[]{:S(2)}, u32[]{:S(2)}) %collective-permute-start.7) | collective-permute-done | bytes 196640 | tf_op jit(solution)/shard_map/ppermute | solution.py:14
  255.5 4.3 %fusion.80 = bf16[128,768]{1,0:T(8,128)(2,1)} fusion(bf16[1,768,1536]{2,1,0:T(8,128)(2,1)S(1)} %copy-done, bf16[1,1536,768]{2,1,0:T(8,128)(2,1)} %param.13, f32[128,1536]{1,0:T(8,128)} %fusion.22, bf16[128,768]{1,0:T(8,128)(2,1)} %collective-permute-done.7, pred[]{:T(512)S(6)} %eq.5, bf16[2,128,768]{2,1,0:T(8,128)(2,1)S(1)} %copy-done.2), kind=kOutput, calls=%fused_computation.76 | convolution fusion | flops 607911936 | bytes 6094849 | tf_op jit(solution)/shard_map/dot_general | solution.py:77
  261.1 1.0 bitcast_dynamic-update-slice_fusion.13
  262.1 1.0 bitcast_dynamic-update-slice_fusion.12
  265.1 1.9 all_gather.19
  267.8 10.4 %all-reduce.14.cloned.1.call-done = bf16[128,768]{1,0:T(8,128)(2,1)} async-done(((bf16[128,768]{1,0:T(8,128)(2,1)}), bf16[128,768]{1,0:T(8,128)(2,1)}) %all-reduce.14.cloned.1.call-update) | async-done | bytes 196624 | tf_op jit(solution)/shard_map/psum | solution.py:80
  278.2 1.1 fusion.311
  279.4 1.4 bitcast_dynamic-update-slice_fusion
  280.8 39.1 %reduce-scatter.18.cloned.1.call-done = bf16[1,1,192,1536]{3,2,1,0:T(8,128)(2,1)} async-done(((bf16[1,1,768,1536]{3,2,1,0:T(8,128)(2,1)}), bf16[1,1,192,1536]{3,2,1,0:T(8,128)(2,1)}) %reduce-scatter.18.cloned.1.call-update) | async-done | bytes 589840 | tf_op jit(solution)/shard_map/reduce_scatter | solution.py:104
  319.9 2.6 bitcast_subtract_fusion.1
  322.5 37.8 %reduce-scatter.20.cloned.1.call-done = bf16[1,1,384,768]{3,2,1,0:T(8,128)(2,1)} async-done(((bf16[1,1,1536,768]{3,2,1,0:T(8,128)(2,1)}), bf16[1,1,384,768]{3,2,1,0:T(8,128)(2,1)}) %reduce-scatter.20.cloned.1.call-update) | async-done | bytes 589840 | tf_op jit(solution)/shard_map/reduce_scatter | solution.py:110
  360.2 2.6 bitcast_subtract_fusion
  (122 shorter events, 15.4 us)
Async XLA Ops:
  7.2 2.3 copy-start
  7.2 16.1 %reduce-scatter.8.cloned.1.call-start = ((), (), s32[]{:S(2)}) async-start(), calls=%async_computation.7 | async-start | bytes 294912 | tf_op jit(solution)/shard_map/reduce_scatter | solution.py:48
  9.5 25.0 %copy-start.1 = (bf16[2,128,768]{2,1,0:T(8,128)(2,1)S(1)}, bf16[2,128,768]{2,1,0:T(8,128)(2,1)}, u32[]{:S(2)}) copy-start(bf16[2,128,768]{2,1,0:T(8,128)(2,1)} %param.9) | copy-start | bytes 1179652
  12.9 36.0 %reduce-scatter.10.cloned.1.call-start = ((), (), s32[]{:S(2)}) async-start(), calls=%async_computation.8 | async-start | bytes 294912 | tf_op jit(solution)/shard_map/reduce_scatter | solution.py:48
  26.2 4.3 %copy-start.4 = (bf16[128,768]{1,0:T(8,128)(2,1)}, bf16[128,768]{1,0:T(8,128)(2,1)S(1)}, u32[]{:S(2)}) copy-start(bf16[128,768]{1,0:T(8,128)(2,1)S(1)} %all_gather.15) | copy-start | bytes 589828
  26.2 8.3 %collective-permute-start = (bf16[128,768]{1,0:T(8,128)(2,1)S(1)}, bf16[128,768]{1,0:T(8,128)(2,1)}, u32[]{:S(2)}, u32[]{:S(2)}) collective-permute-start(bf16[128,768]{1,0:T(8,128)(2,1)S(1)} %all_gather.15), channel_id=1, source_target_pairs={{0,8},{8,16},{16,24},{1,9},{9,17},{17,25},{2,10},{10,18},{18,26},{... | collective-permute-start | bytes 589832 | tf_op jit(solution)/shard_map/ppermute | solution.py:14
  38.2 36.2 %reduce-scatter.12.cloned.1.call-start = ((), (), s32[]{:S(2)}) async-start(), calls=%async_computation.9 | async-start | bytes 294912 | tf_op jit(solution)/shard_map/reduce_scatter | solution.py:48
  51.7 4.3 %copy-start.5 = (bf16[128,768]{1,0:T(8,128)(2,1)}, bf16[128,768]{1,0:T(8,128)(2,1)S(1)}, u32[]{:S(2)}) copy-start(bf16[128,768]{1,0:T(8,128)(2,1)S(1)} %all_gather.16) | copy-start | bytes 589828
  51.8 8.2 %collective-permute-start.1 = (bf16[128,768]{1,0:T(8,128)(2,1)S(1)}, bf16[128,768]{1,0:T(8,128)(2,1)}, u32[]{:S(2)}, u32[]{:S(2)}) collective-permute-start(bf16[128,768]{1,0:T(8,128)(2,1)S(1)} %all_gather.16), channel_id=1, source_target_pairs={{0,8},{8,16},{16,24},{1,9},{9,17},{17,25},{2,10},{10,18},{18,26},{... | collective-permute-start | bytes 589832 | tf_op jit(solution)/shard_map/ppermute | solution.py:14
  63.8 36.2 %reduce-scatter.14.cloned.1.call-start = ((), (), s32[]{:S(2)}) async-start(), calls=%async_computation.10 | async-start | bytes 294912 | tf_op jit(solution)/shard_map/reduce_scatter | solution.py:48
  77.3 4.3 %copy-start.6 = (bf16[128,768]{1,0:T(8,128)(2,1)}, bf16[128,768]{1,0:T(8,128)(2,1)S(1)}, u32[]{:S(2)}) copy-start(bf16[128,768]{1,0:T(8,128)(2,1)S(1)} %all_gather.17) | copy-start | bytes 589828
  77.3 8.2 %collective-permute-start.2 = (bf16[128,768]{1,0:T(8,128)(2,1)S(1)}, bf16[128,768]{1,0:T(8,128)(2,1)}, u32[]{:S(2)}, u32[]{:S(2)}) collective-permute-start(bf16[128,768]{1,0:T(8,128)(2,1)S(1)} %all_gather.17), channel_id=1, source_target_pairs={{0,8},{8,16},{16,24},{1,9},{9,17},{17,25},{2,10},{10,18},{18,26},{... | collective-permute-start | bytes 589832 | tf_op jit(solution)/shard_map/ppermute | solution.py:14
  89.3 50.6 %all-reduce.6.cloned.1.call-start = ((), (), s32[]{:S(2)}) async-start(), calls=%async_computation.12 | async-start | bytes 393216 | tf_op jit(solution)/shard_map/psum | solution.py:80
  102.9 8.5 %copy-start.7 = (bf16[128,768]{1,0:T(8,128)(2,1)}, bf16[128,768]{1,0:T(8,128)(2,1)S(1)}, u32[]{:S(2)}) copy-start(bf16[128,768]{1,0:T(8,128)(2,1)S(1)} %all_gather.18) | copy-start | bytes 589828
  102.9 8.3 %collective-permute-start.3 = (bf16[128,768]{1,0:T(8,128)(2,1)S(1)}, bf16[128,768]{1,0:T(8,128)(2,1)}, u32[]{:S(2)}, u32[]{:S(2)}) collective-permute-start(bf16[128,768]{1,0:T(8,128)(2,1)S(1)} %all_gather.18), channel_id=1, source_target_pairs={{0,8},{8,16},{16,24},{1,9},{9,17},{17,25},{2,10},{10,18},{18,26},{... | collective-permute-start | bytes 589832 | tf_op jit(solution)/shard_map/ppermute | solution.py:14
  111.2 0.7 copy-start.3
  111.9 0.8 copy-start.13
  111.9 2.7 copy-start.2
  113.0 27.0 %copy-start.10 = (f32[128]{0:T(128)}, f32[128]{0:T(128)S(1)}, u32[]{:S(2)}) copy-start(f32[128]{0:T(128)S(1)} %broadcast_multiply_fusion.14) | copy-start | bytes 1540
  113.2 26.8 %copy-start.12 = (f32[128]{0:T(128)}, f32[128]{0:T(128)S(1)}, u32[]{:S(2)}) copy-start(f32[128]{0:T(128)S(1)} %add_rsqrt_fusion.4) | copy-start | bytes 1540
  118.8 56.2 %all-reduce.8.cloned.1.call-start = ((), (), s32[]{:S(2)}) async-start(), calls=%async_computation.13 | async-start | bytes 393216 | tf_op jit(solution)/shard_map/psum | solution.py:80
  118.9 23.0 %copy-start.9 = (f32[128]{0:T(128)}, f32[128]{0:T(128)S(1)}, u32[]{:S(2)}) copy-start(f32[128]{0:T(128)S(1)} %broadcast_multiply_fusion.11) | copy-start | bytes 1540
  141.9 4.6 %copy-start.11 = (f32[128]{0:T(128)}, f32[128]{0:T(128)S(1)}, u32[]{:S(2)}) copy-start(f32[128]{0:T(128)S(1)} %add_rsqrt_fusion.3) | copy-start | bytes 1540
  143.2 9.1 %collective-permute-start.4 = (bf16[128,768]{1,0:T(8,128)(2,1)S(1)}, bf16[128,768]{1,0:T(8,128)(2,1)}, u32[]{:S(2)}, u32[]{:S(2)}) collective-permute-start(bf16[128,768]{1,0:T(8,128)(2,1)S(1)} %get-tuple-element.30), channel_id=1, source_target_pairs={{8,0},{16,8},{24,16},{9,1},{17,9},{25,17},{10,2},{18,10},{26,18},{... | collective-permute-start | bytes 589832 | tf_op jit(solution)/shard_map/ppermute | solution.py:14
  156.5 52.9 %all-reduce.10.cloned.1.call-start = ((), (), s32[]{:S(2)}) async-start(), calls=%async_computation.14 | async-start | bytes 393216 | tf_op jit(solution)/shard_map/psum | solution.py:80
  177.6 9.1 %collective-permute-start.5 = (bf16[128,768]{1,0:T(8,128)(2,1)S(1)}, bf16[128,768]{1,0:T(8,128)(2,1)}, u32[]{:S(2)}, u32[]{:S(2)}) collective-permute-start(bf16[128,768]{1,0:T(8,128)(2,1)S(1)} %get-tuple-element.28), channel_id=1, source_target_pairs={{8,0},{16,8},{24,16},{9,1},{17,9},{25,17},{10,2},{18,10},{26,18},{... | collective-permute-start | bytes 589832 | tf_op jit(solution)/shard_map/ppermute | solution.py:14
  190.9 52.9 %all-reduce.12.cloned.1.call-start = ((), (), s32[]{:S(2)}) async-start(), calls=%async_computation.15 | async-start | bytes 393216 | tf_op jit(solution)/shard_map/psum | solution.py:80
  212.0 9.1 %collective-permute-start.6 = (bf16[128,768]{1,0:T(8,128)(2,1)S(1)}, bf16[128,768]{1,0:T(8,128)(2,1)}, u32[]{:S(2)}, u32[]{:S(2)}) collective-permute-start(bf16[128,768]{1,0:T(8,128)(2,1)S(1)} %get-tuple-element.26), channel_id=1, source_target_pairs={{8,0},{16,8},{24,16},{9,1},{17,9},{25,17},{10,2},{18,10},{26,18},{... | collective-permute-start | bytes 589832 | tf_op jit(solution)/shard_map/ppermute | solution.py:14
  215.3 10.1 %copy-start.14 = (f32[128]{0:T(128)S(1)}, f32[128]{0:T(128)}, u32[]{:S(2)}) copy-start(f32[128]{0:T(128)} %copy-done.13) | copy-start | bytes 1540
  225.3 38.8 %reduce-scatter.16.cloned.1.call-start = ((), (), s32[]{:S(2)}) async-start(), calls=%async_computation.11 | async-start | bytes 294912 | tf_op jit(solution)/shard_map/reduce_scatter | solution.py:48
  228.9 49.3 %all-reduce.14.cloned.1.call-start = ((), (), s32[]{:S(2)}) async-start(), calls=%async_computation.16 | async-start | bytes 393216 | tf_op jit(solution)/shard_map/psum | solution.py:80
  246.4 9.1 %collective-permute-start.7 = (bf16[128,768]{1,0:T(8,128)(2,1)S(1)}, bf16[128,768]{1,0:T(8,128)(2,1)}, u32[]{:S(2)}, u32[]{:S(2)}) collective-permute-start(bf16[128,768]{1,0:T(8,128)(2,1)S(1)} %get-tuple-element.24), channel_id=1, source_target_pairs={{8,0},{16,8},{24,16},{9,1},{17,9},{25,17},{10,2},{18,10},{26,18},{... | collective-permute-start | bytes 589832 | tf_op jit(solution)/shard_map/ppermute | solution.py:14
  259.8 60.1 %reduce-scatter.18.cloned.1.call-start = ((), (), s32[]{:S(2)}) async-start(), calls=%async_computation.17 | async-start | bytes 2949120 | tf_op jit(solution)/shard_map/reduce_scatter | solution.py:104
  260.5 99.7 %reduce-scatter.20.cloned.1.call-start = ((), (), s32[]{:S(2)}) async-start(), calls=%async_computation.18 | async-start | bytes 2949120 | tf_op jit(solution)/shard_map/reduce_scatter | solution.py:110
  280.7 82.0 %copy-start.8 = (bf16[1,2,128,768]{3,2,1,0:T(8,128)(2,1)}, bf16[1,2,128,768]{3,2,1,0:T(8,128)(2,1)S(1)}, u32[]{:S(2)}) copy-start(bf16[1,2,128,768]{3,2,1,0:T(8,128)(2,1)S(1)} %bitcast_dynamic-update-slice_fusion) | copy-start | bytes 1179652
Sparse Core Ops, SparseCore 0:
  13.0 10.2 reduce-scatter.7
  38.3 10.4 reduce-scatter.9
  63.9 10.4 reduce-scatter.11
  89.5 10.4 reduce-scatter.13
  118.9 20.9 all-reduce.5
  156.7 18.2 all-reduce.7
  191.1 18.2 all-reduce.9
  225.5 18.2 all-reduce.11
  246.0 8.7 reduce-scatter.15
  259.9 18.2 all-reduce.13
  281.3 38.5 reduce-scatter.17
  322.8 37.3 reduce-scatter.19
where the time goes:
time: 371 us; the launch traced here: 370 us
  waiting for transfers between devices  238 us (64%)
  matrix products  47 us (13%)
  other arithmetic  33.6 us (9%)
  starting transfers between devices  23 us (6%)
  between operations  14.7 us (4%)
  blocking collectives  9.74 us (3%)
    psum x5, waiting for transfers between devices, layer_backward(): lax.psum(partial_value.astype(jnp.bfloat16), 'tensor').astype(jnp.float32)  78.9 us
    reduce_scatter x5, waiting for transfers between devices, layer_forward(): lax.psum_scatter(partial_value.astype(jnp.bfloat16), 'tensor', scatter_di...  42.2 us
    reduce_scatter x1, waiting for transfers between devices, local(): lax.psum_scatter(prior_up_grad.astype(jnp.float32).astype(jnp.bfloat16),...  39.1 us
    ppermute x8, waiting for transfers between devices, shifted(): lax.ppermute(value, axis, [(source, source + steps) for source in range(i...  38.5 us
    reduce_scatter x1, waiting for transfers between devices, local(): lax.psum_scatter(prior_down_grad.astype(jnp.float32).astype(jnp.bfloat16)...  37.8 us
    ppermute x8, starting transfers between devices, shifted(): lax.ppermute(value, axis, [(source, source + steps) for source in range(i...  22.6 us
    dot_general x5, matrix products, layer_backward(): lax.dot_general(grad_up, w_up, (((1,), (1,)), ((), ())), preferred_elemen...  21.2 us
    dot_general x5, matrix products, layer_forward(): partial_value = jnp.dot(active, w_down, preferred_element_type=jnp.float32)  16.8 us
  transfers between devices with their start and end apart: 20, of which 19 were waited for; matrix products, arithmetic and copies ran while one was open for 9% of the time, Pallas kernels for 0%

commit v1 on v0

v1 whole, which is shorter than its diff:
```python
import functools

import jax
import jax.numpy as jnp
from jax import lax
from jax.experimental import pallas as pl
from jax.experimental.pallas import tpu as pltpu
from jax.sharding import PartitionSpec as P

eps_norm = 1e-05
gelu_coef = 0.7978845608028654
learning_rate = 0.05
MESH = pl.DeviceIdType.MESH
NT = (((1,), (1,)), ((), ()))


def flipped(index, bit):
    return index + bit - 2 * bit * (lax.rem(index // bit, 2))


def row_step(rows):
    for step in (64, 32, 16):
        if rows % step == 0:
            return step
    return rows


def subsets(bits):
    if not bits:
        return [0]
    rest = subsets(bits[1:])
    return [bits[0] + r for r in rest] + rest


class Halving:
    def __init__(self, bits, source, acc, recv, total, load_sem, send_sem, recv_sem, me):
        self.bits, self.source, self.acc, self.recv, self.total = bits, source, acc, recv, total
        self.load_sem, self.send_sem, self.recv_sem, self.me = load_sem, send_sem, recv_sem, me
        self.kept = subsets(bits[1:])
        self.slots = [(p, q) for p in range(len(bits)) for q in subsets(bits[p + 1 :])]

    def block(self, rel):
        index = self.me
        for bit in self.bits:
            if rel & bit:
                index = flipped(index, bit)
        return index

    def copy(self, slot):
        p, q = self.slots[slot]
        rel = q + self.bits[p]
        src = self.source.at[self.block(rel)] if p == 0 else self.acc.at[self.kept.index(rel)]
        return pltpu.make_async_remote_copy(
            src_ref=src,
            dst_ref=self.recv.at[slot],
            send_sem=self.send_sem.at[slot],
            recv_sem=self.recv_sem.at[slot],
            device_id={"dp": flipped(self.me, self.bits[p])},
            device_id_type=MESH,
        )

    def load(self, k):
        return pltpu.make_async_copy(
            self.source.at[self.block(self.kept[k])], self.acc.at[k], self.load_sem.at[k]
        )

    def begin(self):
        for slot, (p, _) in enumerate(self.slots):
            if p == 0:
                self.copy(slot).start()
        for k in range(len(self.kept)):
            self.load(k).start()

    def event(self, slot):
        p, q = self.slots[slot]
        k = self.kept.index(q)
        if p == 0:
            self.load(k).wait()
        self.copy(slot).wait_recv()
        last = p == len(self.bits) - 1
        rows = self.acc.shape[1]
        step = row_step(rows)

        def body(i):
            at = pl.ds(pl.multiple_of(i * step, step), step)
            summed = self.acc[k, at, :].astype(jnp.float32) + self.recv[slot, at, :].astype(jnp.float32)
            if last:
                self.total[at, :] = summed
            else:
                self.acc[k, at, :] = summed.astype(jnp.bfloat16)

        if rows == step:
            summed = self.acc[k].astype(jnp.float32) + self.recv[slot].astype(jnp.float32)
            if last:
                self.total[...] = summed
            else:
                self.acc[k] = summed.astype(jnp.bfloat16)
        else:
            pl.loop(0, rows // step)(body)
        if not last and q & self.bits[p + 1]:
            self.copy(self.slots.index((p + 1, q - self.bits[p + 1]))).start()

    def finish(self):
        for slot in range(len(self.slots)):
            self.copy(slot).wait_send()


def window_kernel(
    ns, n, nt, chunk,
    x_hbm, g_hbm, gain_ref, up_hbm, down_hbm, pu_hbm, pd_hbm,
    outs_hbm, grads_hbm, tu_ref, td_ref,
    up_v, down_v, xin, gin, ybuf, zbuf, act, slope, xhat, rstd,
    acc_u, acc_d, recv_u, recv_d,
    wl_sem, ws_sem, wr_sem, il_sem, hs_sem, hr_sem, ol_sem, os_sem, or_sem,
    rl_sem, rs_sem, rr_sem,
):
    sec = lax.axis_index("section")
    me = lax.axis_index("dp")
    ten = lax.axis_index("tensor")
    micro, rows = xin.shape[0], xin.shape[1]
    hid = up_v.shape[2]
    bits = [1 << b for b in range(n.bit_length() - 1)]
    my_rows = pl.ds(pl.multiple_of(ten * rows, rows), rows)
    peers = [lax.rem(ten + k, nt) for k in range(1, nt)]
    first, final = sec == 0, sec == ns - 1

    barrier = pltpu.get_barrier_semaphore()
    for peer in peers:
        pl.semaphore_signal(barrier, inc=1, device_id={"tensor": peer}, device_id_type=MESH)
    for bit in bits:
        pl.semaphore_signal(barrier, inc=1, device_id={"dp": flipped(me, bit)}, device_id_type=MESH)

    @pl.when(sec > 0)
    def _():
        pl.semaphore_signal(barrier, inc=1, device_id={"section": sec - 1}, device_id_type=MESH)

    @pl.when(sec < ns - 1)
    def _():
        pl.semaphore_signal(barrier, inc=1, device_id={"section": sec + 1}, device_id_type=MESH)

    own_w = [
        pltpu.make_async_copy(up_hbm, up_v.at[0], wl_sem.at[0]),
        pltpu.make_async_copy(down_hbm, down_v.at[0], wl_sem.at[1]),
    ]
    x_local = [pltpu.make_async_copy(x_hbm.at[m, my_rows, :], xin.at[m], il_sem.at[0, m]) for m in range(micro)]
    g_local = [pltpu.make_async_copy(g_hbm.at[m, my_rows, :], gin.at[m], il_sem.at[1, m]) for m in range(micro)]

    @pl.when(first)
    def _():
        for c in x_local:
            c.start()

    for c in own_w:
        c.start()

    @pl.when(final)
    def _():
        for c in g_local:
            c.start()

    ends = sec // max(ns - 1, 1) + (ns - 1 - sec) // max(ns - 1, 1) if ns > 1 else 2
    pl.semaphore_wait(barrier, len(peers) + len(bits) + 2 - ends)

    def w_copy(which, k):
        src, dst = ((up_hbm, up_v), (down_hbm, down_v))[which]
        return pltpu.make_async_remote_copy(
            src_ref=src,
            dst_ref=dst.at[k],
            send_sem=ws_sem.at[which, k - 1],
            recv_sem=wr_sem.at[which, k - 1],
            device_id={"tensor": peers[k - 1]},
            device_id_type=MESH,
        )

    for which in range(2):
        for k in range(1, nt):
            w_copy(which, k).start()

    streams = (
        Halving(bits, pu_hbm, acc_u, recv_u, tu_ref, rl_sem.at[0], rs_sem.at[0], rr_sem.at[0], me),
        Halving(bits[::-1], pd_hbm, acc_d, recv_d, td_ref, rl_sem.at[1], rs_sem.at[1], rr_sem.at[1], me),
    )
    for stream in streams:
        stream.begin()

    def hop(back, m):
        return pltpu.make_async_remote_copy(
            src_ref=(zbuf if back else ybuf).at[m],
            dst_ref=(gin if back else xin).at[m],
            send_sem=hs_sem.at[back, m],
            recv_sem=hr_sem.at[back, m],
            device_id={"section": sec - 1 if back else sec + 1},
            device_id_type=MESH,
        )

    def out_local(back, m):
        src, dst = ((ybuf, outs_hbm), (zbuf, grads_hbm))[back]
        return pltpu.make_async_copy(src.at[m], dst.at[m, my_rows, :], ol_sem.at[back, m])

    def out_remote(back, m, k):
        src, dst = ((ybuf, outs_hbm), (zbuf, grads_hbm))[back]
        return pltpu.make_async_remote_copy(
            src_ref=src.at[m],
            dst_ref=dst.at[m, my_rows, :],
            send_sem=os_sem.at[back, m, k - 1],
            recv_sem=or_sem.at[back, m, k - 1],
            device_id={"tensor": peers[k - 1]},
            device_id_type=MESH,
        )

    def give(back, m):
        out_local(back, m).start()
        for k in range(1, nt):
            out_remote(back, m, k).start()

    gain = gain_ref[...]
    cuts = [slice(c, c + chunk) for c in range(0, hid, chunk)]

    for m in range(micro):
        @pl.when(first)
        def _():
            x_local[m].wait()

        @pl.when(sec > 0)
        def _():
            hop(0, m).wait_recv()

        values = xin[m].astype(jnp.float32)
        center = jnp.mean(values, axis=-1, keepdims=True)
        centered = values - center
        spread = jnp.mean(centered * centered, axis=-1, keepdims=True)
        scale = lax.rsqrt(spread + eps_norm)
        standard = centered * scale
        xhat[m] = standard
        rstd[m] = jnp.broadcast_to(scale, rstd.shape[1:])
        normed = (standard * gain).astype(jnp.bfloat16)
        for k in range(nt):
            if m == 0:
                if k == 0:
                    own_w[0].wait()
                else:
                    w_copy(0, k).wait_recv()
            for cut in cuts:
                u = jnp.dot(normed, up_v[k, :, cut], preferred_element_type=jnp.float32)
                t = jnp.tanh(gelu_coef * (u + 0.044715 * u * u * u))
                act[k, :, cut] = (0.5 * u * (1.0 + t)).astype(jnp.bfloat16)
                slope[m, k, :, cut] = 0.5 * (1.0 + t) + 0.5 * u * (1.0 - t * t) * gelu_coef * (
                    1.0 + 3.0 * 0.044715 * u * u
                )
        mixed = None
        for k in range(nt):
            if m == 0:
                if k == 0:
                    own_w[1].wait()
                else:
                    w_copy(1, k).wait_recv()
            term = jnp.dot(act[k], down_v[k], preferred_element_type=jnp.float32)
            mixed = term if mixed is None else mixed + term
        ybuf[m] = (xin[m].astype(jnp.float32) + mixed).astype(jnp.bfloat16)

        @pl.when(sec < ns - 1)
        def _():
            hop(0, m).start()

        give(0, m)

    count = len(streams[0].slots)
    early = max(1, count // 3)
    middle = max(early, count - 1)
    for slot in range(early):
        for stream in streams:
            stream.event(slot)

    @pl.when(sec < ns - 2)
    def _():
        for slot in range(early, middle):
            for stream in streams:
                stream.event(slot)

    for m in range(micro):
        @pl.when(final)
        def _():
            g_local[m].wait()

        @pl.when(sec < ns - 1)
        def _():
            hop(1, m).wait_recv()

        g = gin[m]
        for k in range(nt):
            for cut in cuts:
                ga = lax.dot_general(g, down_v[k, cut, :], NT, preferred_element_type=jnp.float32)
                act[k, :, cut] = (ga * slope[m, k, :, cut]).astype(jnp.bfloat16)
        gn = None
        for k in range(nt):
            term = lax.dot_general(act[k], up_v[k], NT, preferred_element_type=jnp.float32)
            gn = term if gn is None else gn + term
        standard = xhat[m]
        dn = gn * gain
        lead = jnp.mean(dn, axis=-1, keepdims=True)
        trail = jnp.mean(dn * standard, axis=-1, keepdims=True)
        zbuf[m] = (
            gin[m].astype(jnp.float32) + rstd[m][:, :1] * (dn - lead - standard * trail)
        ).astype(jnp.bfloat16)

        @pl.when(sec > 0)
        def _():
            hop(1, m).start()

        give(1, m)

    @pl.when(sec >= ns - 2)
    def _():
        for slot in range(early, middle):
            for stream in streams:
                stream.event(slot)

    for slot in range(middle, count):
        for stream in streams:
            stream.event(slot)

    for stream in streams:
        stream.finish()
    for which in range(2):
        for k in range(1, nt):
            w_copy(which, k).wait_send()
    for m in range(micro):
        @pl.when(sec < ns - 1)
        def _():
            hop(0, m).wait_send()

        @pl.when(sec > 0)
        def _():
            hop(1, m).wait_send()

        for back in range(2):
            out_local(back, m).wait()
            for k in range(1, nt):
                out_remote(back, m, k).wait_send()
                out_remote(back, m, k).wait_recv()


def local(
    ns, n, nt,
    inputs, out_grads, norm_gain, up_weight, down_weight,
    prior_up_grad, prior_down_grad, master_up, master_down,
):
    micro, tokens, d = inputs.shape
    rows = tokens // nt
    hid = up_weight.shape[2]
    chunk = next((c for c in (512, 256, 128) if hid % c == 0), hid)
    pu = prior_up_grad.reshape(n, d // n, hid)
    pd = prior_down_grad.reshape(n, hid // n, d)
    bf, f32 = jnp.bfloat16, jnp.float32
    vm, dma = pltpu.VMEM, pltpu.SemaphoreType.DMA
    k = max(nt - 1, 1)
    anywhere = pl.BlockSpec(memory_space=pl.ANY)
    inside = pl.BlockSpec(memory_space=pltpu.VMEM)
    macs = micro * rows * d * hid * nt * 4
    outs, grads, total_up, total_down = pl.pallas_call(
        functools.partial(window_kernel, ns, n, nt, chunk),
        out_shape=(
            jax.ShapeDtypeStruct((micro, tokens, d), bf),
            jax.ShapeDtypeStruct((micro, tokens, d), bf),
            jax.ShapeDtypeStruct((d // n, hid), f32),
            jax.ShapeDtypeStruct((hid // n, d), f32),
        ),
        in_specs=[anywhere, anywhere, inside] + [anywhere] * 4,
        out_specs=(anywhere, anywhere, inside, inside),
        scratch_shapes=[
            vm((nt, d, hid), bf),
            vm((nt, hid, d), bf),
            vm((micro, rows, d), bf),
            vm((micro, rows, d), bf),
            vm((micro, rows, d), bf),
            vm((micro, rows, d), bf),
            vm((nt, rows, hid), bf),
            vm((micro, nt, rows, hid), f32),
            vm((micro, rows, d), f32),
            vm((micro, rows, 128), f32),
            vm((n // 2, d // n, hid), bf),
            vm((n // 2, hid // n, d), bf),
            vm((n - 1, d // n, hid), bf),
            vm((n - 1, hid // n, d), bf),
            dma((2,)), dma((2, k)), dma((2, k)),
            dma((2, micro)), dma((2, micro)), dma((2, micro)),
            dma((2, micro)), dma((2, micro, k)), dma((2, micro, k)),
            dma((2, n // 2)), dma((2, n - 1)), dma((2, n - 1)),
        ],
        compiler_params=pltpu.CompilerParams(
            collective_id=0, has_side_effects=True, vmem_limit_bytes=48 * 1024 * 1024
        ),
        cost_estimate=pl.CostEstimate(flops=2 * macs, bytes_accessed=4 * hid * d * 4, transcendentals=micro * rows * hid * nt),
        name="window",
    )(inputs, out_grads, norm_gain, up_weight[0], down_weight[0], pu, pd)
    new_up = master_up[0] - learning_rate * total_up
    new_down = master_down[0] - learning_rate * total_down
    return (outs[None], grads[None], new_up[None], new_down[None])


def solution(mesh):
    placed = (
        P(None, "dp", None),
        P(None, "dp", None),
        P("section", None),
        P("section", None, "tensor"),
        P("section", "tensor", None),
        P("dp", "section", None, "tensor"),
        P("dp", "section", "tensor", None),
        P("section", "dp", "tensor"),
        P("section", ("tensor", "dp"), None),
    )
    sizes = (mesh.shape["section"], mesh.shape["dp"], mesh.shape["tensor"])
    return jax.shard_map(
        functools.partial(local, *sizes),
        mesh=mesh,
        in_specs=placed,
        out_specs=(
            P("section", None, "dp", None),
            P("section", None, "dp", None),
            P("section", "dp", "tensor"),
            P("section", ("tensor", "dp"), None),
        ),
        check_vma=False,
    )
```

time: 371 us -> 72.9 us (0.20)
  waiting for transfers between devices: 238 us -> 0 us
  Pallas kernels: 0 us -> 64.8 us
  matrix products: 47 us -> 0 us
  other arithmetic: 33.6 us -> 2.45 us
  starting transfers between devices: 23 us -> 0 us
  between operations: 14.7 us -> 0.67 us
  blocking collectives: 9.74 us -> 0 us
    reduce_scatter x7 -> x0, waiting for transfers between devices: 119 us -> none  [the longest x5 42.2 us: layer_forward(): lax.psum_scatter(partial_value.astype(jnp.bfloat16), 'tensor', scatter_di...]
    psum x5 -> x0, waiting for transfers between devices: 78.9 us -> none  [layer_backward(): lax.psum(partial_value.astype(jnp.bfloat16), 'tensor').astype(jnp.float32)]
    pallas_call x0 -> x1, Pallas kernels: none -> 64.8 us  [local(): pl.pallas_call(functools.partial(window_kernel, ns, n, nt, chunk), out_sh...]
    dot_general x15 -> x0, matrix products: 47 us -> none  [the longest x5 21.2 us: layer_backward(): lax.dot_general(grad_up, w_up, (((1,), (1,)), ((), ())), preferred_elemen...]
    ppermute x8 -> x0, waiting for transfers between devices: 38.5 us -> none  [shifted(): lax.ppermute(value, axis, [(source, source + steps) for source in range(i...]
    ppermute x8 -> x0, starting transfers between devices: 22.6 us -> none  [shifted(): lax.ppermute(value, axis, [(source, source + steps) for source in range(i...]
    dynamic_update_slice x15 -> x0, other arithmetic: 11 us -> none  [store_row(): return lax.dynamic_update_index_in_dim(buffer, chosen, slot_index, 0)]
    all_gather x5 -> x0, blocking collectives: 9.74 us -> none  [layer_forward(): return lax.all_gather(half_out, 'tensor', axis=0, tiled=True)]
  transfers between devices with their start and end apart: 20 -> 0, of which waited for: 19 -> 0; matrix products, arithmetic and copies ran while one was open for 9% -> 0% of each run, Pallas kernels for 0% -> 0%
where the time goes in v1:
time: 72.9 us; the launch traced here: 72.6 us
  Pallas kernels  64.8 us (89%)
  local copies, waits for them, and re-layouts  4.69 us (6%)
  other arithmetic  2.45 us (3%)
    pallas_call x1, Pallas kernels, local(): pl.pallas_call(functools.partial(window_kernel, ns, n, nt, chunk), out_sh...  64.8 us
    unnamed x12, local copies, waits for them, and re-layouts  4.69 us
    broadcast_in_dim x2, other arithmetic, local(): return (outs[None], grads[None], new_up[None], new_down[None])  2.45 us

profile of v1, /device:TPU:0, one launch (start us, length us, event | category | flops | bytes accessed | tf_op | source)
XLA Modules:
  0.0 72.6 jit_solution(6966617500937739725)
XLA Ops:
  0.6 0.0 copy-start
  0.6 1.0 %copy-done = bf16[2,128,768]{2,1,0:T(8,128)(2,1)S(1)} copy-done((bf16[2,128,768]{2,1,0:T(8,128)(2,1)S(1)}, bf16[2,128,768]{2,1,0:T(8,128)(2,1)}, u32[]{:S(2)}) %copy-start) | copy-done | bytes 393240
  1.6 0.0 copy-start.1
  1.6 1.0 %copy-done.1 = bf16[2,128,768]{2,1,0:T(8,128)(2,1)S(1)} copy-done((bf16[2,128,768]{2,1,0:T(8,128)(2,1)S(1)}, bf16[2,128,768]{2,1,0:T(8,128)(2,1)}, u32[]{:S(2)}) %copy-start.1) | copy-done | bytes 393240
  2.6 0.0 copy-start.2
  2.6 0.7 copy-done.2
  3.3 0.0 copy-start.3
  3.3 64.8 %window.1 = (bf16[2,128,768]{2,1,0:T(8,128)(2,1)S(1)}, bf16[2,128,768]{2,1,0:T(8,128)(2,1)S(1)}, f32[192,1536]{1,0:T(8,128)S(1)}, f32[384,768]{1,0:T(8,128)S(1)}) custom-call(bf16[2,128,768]{2,1,0:T(8,128)(2,1)S(1)} %copy-done, bf16[2,128,768]{2,1,0:T(8,128)(2,1)S(1)} %copy-done.1, f32[1,768]{1,0:T(1,128)S(1)} %copy-done.2, bf16[768,1536]{1,0:T(8,128)(2,1)} %bitcast.20, ...), custom_call_target="tpu_custom_call" | custom-call | flops 2415919104 | bytes 18874368 | tf_op jit(solution)/shard_map/window/pallas_call | solution.py:360
  68.1 0.0 copy-done.3
  68.1 0.0 copy-start.4
  68.1 1.2 %fusion.1 = f32[1,192,1536]{2,1,0:T(8,128)} fusion(f32[1,192,1536]{2,1,0:T(8,128)S(1)} %copy-done.3, f32[192,1536]{1,0:T(8,128)S(1)} %get-tuple-element.10), kind=kLoop, calls=%fused_computation.3 | loop fusion | flops 589824 | bytes 3538944 | tf_op jit(solution)/shard_map/broadcast_in_dim | solution.py:398
  69.3 0.5 copy-done.4
  69.8 1.3 %fusion = f32[1,384,768]{2,1,0:T(8,128)} fusion(f32[1,384,768]{2,1,0:T(8,128)S(1)} %copy-done.4, f32[384,768]{1,0:T(8,128)S(1)} %get-tuple-element.11), kind=kLoop, calls=%fused_computation.1 | loop fusion | flops 589824 | bytes 3538944 | tf_op jit(solution)/shard_map/broadcast_in_dim | solution.py:398
  71.1 0.7 %copy.15 = bf16[1,2,128,768]{3,2,1,0:T(8,128)(2,1)} copy(bf16[1,2,128,768]{3,2,1,0:T(8,128)(2,1)S(1)} %bitcast.19) | data formatting | bytes 786432
  71.9 0.7 %copy.16 = bf16[1,2,128,768]{3,2,1,0:T(8,128)(2,1)} copy(bf16[1,2,128,768]{3,2,1,0:T(8,128)(2,1)S(1)} %bitcast.18) | data formatting | bytes 786432
Async XLA Ops:
  0.6 1.0 %copy-start = (bf16[2,128,768]{2,1,0:T(8,128)(2,1)S(1)}, bf16[2,128,768]{2,1,0:T(8,128)(2,1)}, u32[]{:S(2)}) copy-start(bf16[2,128,768]{2,1,0:T(8,128)(2,1)} %x_hbm.1) | copy-start | bytes 1179652
  1.6 1.0 %copy-start.1 = (bf16[2,128,768]{2,1,0:T(8,128)(2,1)S(1)}, bf16[2,128,768]{2,1,0:T(8,128)(2,1)}, u32[]{:S(2)}) copy-start(bf16[2,128,768]{2,1,0:T(8,128)(2,1)} %g_hbm.1) | copy-start | bytes 1179652
  2.6 0.7 copy-start.2
  3.3 64.8 %copy-start.3 = (f32[1,192,1536]{2,1,0:T(8,128)S(1)}, f32[1,192,1536]{2,1,0:T(8,128)}, u32[]{:S(2)}) copy-start(f32[1,192,1536]{2,1,0:T(8,128)} %param.16) | copy-start | bytes 3538948
  68.1 1.7 %copy-start.4 = (f32[1,384,768]{2,1,0:T(8,128)S(1)}, f32[1,384,768]{2,1,0:T(8,128)}, u32[]{:S(2)}) copy-start(f32[1,384,768]{2,1,0:T(8,128)} %param.17) | copy-start | bytes 3538948

commit v2 on v1

--- a/solution.py
+++ b/solution.py
@@ -33,8 +33,9 @@
 
 
 class Halving:
-    def __init__(self, bits, source, acc, recv, total, load_sem, send_sem, recv_sem, me):
+    def __init__(self, bits, source, acc, recv, master, total, load_sem, send_sem, recv_sem, me):
         self.bits, self.source, self.acc, self.recv, self.total = bits, source, acc, recv, total
+        self.master = master
         self.load_sem, self.send_sem, self.recv_sem, self.me = load_sem, send_sem, recv_sem, me
         self.kept = subsets(bits[1:])
         self.slots = [(p, q) for p in range(len(bits)) for q in subsets(bits[p + 1 :])]
@@ -85,14 +86,14 @@
             at = pl.ds(pl.multiple_of(i * step, step), step)
             summed = self.acc[k, at, :].astype(jnp.float32) + self.recv[slot, at, :].astype(jnp.float32)
             if last:
-                self.total[at, :] = summed
+                self.total[at, :] = self.master[at, :] - learning_rate * summed
             else:
                 self.acc[k, at, :] = summed.astype(jnp.bfloat16)
 
         if rows == step:
             summed = self.acc[k].astype(jnp.float32) + self.recv[slot].astype(jnp.float32)
             if last:
-                self.total[...] = summed
+                self.total[...] = self.master[...] - learning_rate * summed
             else:
                 self.acc[k] = summed.astype(jnp.bfloat16)
         else:
@@ -107,11 +108,11 @@
 
 def window_kernel(
     ns, n, nt, chunk,
-    x_hbm, g_hbm, gain_ref, up_hbm, down_hbm, pu_hbm, pd_hbm,
+    x_hbm, g_hbm, gain_hbm, up_hbm, down_hbm, pu_hbm, pd_hbm, mu_hbm, md_hbm,
     outs_hbm, grads_hbm, tu_ref, td_ref,
-    up_v, down_v, xin, gin, ybuf, zbuf, act, slope, xhat, rstd,
+    gain_ref, up_v, down_v, up_t, down_t, master_u, master_d, xall, pall, psend, precv, xin, gin, ybuf, zbuf, act, wide, slope, xhat, rstd,
     acc_u, acc_d, recv_u, recv_d,
-    wl_sem, ws_sem, wr_sem, il_sem, hs_sem, hr_sem, ol_sem, os_sem, or_sem,
+    wl_sem, ml_sem, ps_sem, pr_sem, ws_sem, wr_sem, il_sem, hs_sem, hr_sem, ol_sem, os_sem, or_sem,
     rl_sem, rs_sem, rr_sem,
 ):
     sec = lax.axis_index("section")
@@ -145,8 +146,18 @@
     x_local = [pltpu.make_async_copy(x_hbm.at[m, my_rows, :], xin.at[m], il_sem.at[0, m]) for m in range(micro)]
     g_local = [pltpu.make_async_copy(g_hbm.at[m, my_rows, :], gin.at[m], il_sem.at[1, m]) for m in range(micro)]
 
+    x_whole = [pltpu.make_async_copy(x_hbm.at[m], xall.at[m], il_sem.at[2, m]) for m in range(micro)]
+    own_m = [
+        pltpu.make_async_copy(mu_hbm, master_u, ml_sem.at[0]),
+        pltpu.make_async_copy(md_hbm, master_d, ml_sem.at[1]),
+    ]
+    gain_load = pltpu.make_async_copy(gain_hbm, gain_ref, ml_sem.at[2])
+    gain_load.start()
+
     @pl.when(first)
     def _():
+        for c in x_whole:
+            c.start()
         for c in x_local:
             c.start()
 
@@ -172,16 +183,23 @@
             device_id_type=MESH,
         )
 
-    for which in range(2):
-        for k in range(1, nt):
-            w_copy(which, k).start()
+    def trade():
+        for which in range(2):
+            for k in range(1, nt):
+                w_copy(which, k).start()
+
+    @pl.when(sec > 0)
+    def _():
+        trade()
 
     streams = (
-        Halving(bits, pu_hbm, acc_u, recv_u, tu_ref, rl_sem.at[0], rs_sem.at[0], rr_sem.at[0], me),
-        Halving(bits[::-1], pd_hbm, acc_d, recv_d, td_ref, rl_sem.at[1], rs_sem.at[1], rr_sem.at[1], me),
+        Halving(bits, pu_hbm, acc_u, recv_u, master_u, tu_ref, rl_sem.at[0], rs_sem.at[0], rr_sem.at[0], me),
+        Halving(bits[::-1], pd_hbm, acc_d, recv_d, master_d, td_ref, rl_sem.at[1], rs_sem.at[1], rr_sem.at[1], me),
     )
     for stream in streams:
         stream.begin()
+    for c in own_m:
+        c.start()
 
     def hop(back, m):
         return pltpu.make_async_remote_copy(
@@ -213,33 +231,33 @@
         for k in range(1, nt):
             out_remote(back, m, k).start()
 
+    gain_load.wait()
     gain = gain_ref[...]
     cuts = [slice(c, c + chunk) for c in range(0, hid, chunk)]
 
-    for m in range(micro):
-        @pl.when(first)
-        def _():
-            x_local[m].wait()
-
-        @pl.when(sec > 0)
-        def _():
-            hop(0, m).wait_recv()
-
-        values = xin[m].astype(jnp.float32)
+    def normalized(values):
         center = jnp.mean(values, axis=-1, keepdims=True)
         centered = values - center
         spread = jnp.mean(centered * centered, axis=-1, keepdims=True)
         scale = lax.rsqrt(spread + eps_norm)
-        standard = centered * scale
+        return centered * scale, scale
+
+    def part(m, k):
+        return pltpu.make_async_remote_copy(
+            src_ref=psend.at[m, k - 1],
+            dst_ref=precv.at[m, k - 1],
+            send_sem=ps_sem.at[m, k - 1],
+            recv_sem=pr_sem.at[m, k - 1],
+            device_id={"tensor": peers[k - 1]},
+            device_id_type=MESH,
+        )
+
+    def front(m):
+        standard, scale = normalized(xin[m].astype(jnp.float32))
         xhat[m] = standard
         rstd[m] = jnp.broadcast_to(scale, rstd.shape[1:])
         normed = (standard * gain).astype(jnp.bfloat16)
         for k in range(nt):
-            if m == 0:
-                if k == 0:
-                    own_w[0].wait()
-                else:
-                    w_copy(0, k).wait_recv()
             for cut in cuts:
                 u = jnp.dot(normed, up_v[k, :, cut], preferred_element_type=jnp.float32)
                 t = jnp.tanh(gelu_coef * (u + 0.044715 * u * u * u))
@@ -247,35 +265,109 @@
                 slope[m, k, :, cut] = 0.5 * (1.0 + t) + 0.5 * u * (1.0 - t * t) * gelu_coef * (
                     1.0 + 3.0 * 0.044715 * u * u
                 )
-        mixed = None
+
+    def weights_here(own):
+        if own:
+            for c in own_w:
+                c.wait()
+        for which in range(2):
+            for k in range(1, nt):
+                w_copy(which, k).wait_recv()
+
+    tile = next((c for c in (256, 128) if hid % c == 0), hid)
+
+    def turn():
         for k in range(nt):
+            @pl.loop(0, hid // tile)
+            def _(i):
+                at = pl.ds(pl.multiple_of(i * tile, tile), tile)
+                down_t[k, :, at] = down_v[k, at, :].T
+                up_t[k, at, :] = up_v[k, :, at].T
+
+    count = len(streams[0].slots)
+
+    def events(start, stop):
+        for slot in range(start, stop):
+            for stream in streams:
+                if slot == count - 1:
+                    own_m[streams.index(stream)].wait()
+                stream.event(slot)
+
+    @pl.when(first)
+    def _():
+        for m in range(micro):
+            x_whole[m].wait()
             if m == 0:
-                if k == 0:
-                    own_w[1].wait()
-                else:
-                    w_copy(1, k).wait_recv()
-            term = jnp.dot(act[k], down_v[k], preferred_element_type=jnp.float32)
-            mixed = term if mixed is None else mixed + term
-        ybuf[m] = (xin[m].astype(jnp.float32) + mixed).astype(jnp.bfloat16)
-
-        @pl.when(sec < ns - 1)
-        def _():
-            hop(0, m).start()
-
-        give(0, m)
-
-    count = len(streams[0].slots)
-    early = max(1, count // 3)
-    middle = max(early, count - 1)
-    for slot in range(early):
-        for stream in streams:
-            stream.event(slot)
-
-    @pl.when(sec < ns - 2)
-    def _():
-        for slot in range(early, middle):
-            for stream in streams:
-                stream.event(slot)
+                own_w[0].wait()
+            standard, _ = normalized(xall[m].astype(jnp.float32))
+            normed = (standard * gain).astype(jnp.bfloat16)
+            for cut in cuts:
+                u = jnp.dot(normed, up_v[0, :, cut], preferred_element_type=jnp.float32)
+                t = jnp.tanh(gelu_coef * (u + 0.044715 * u * u * u))
+                wide[:, cut] = (0.5 * u * (1.0 + t)).astype(jnp.bfloat16)
+            if m == 0:
+                own_w[1].wait()
+            pall[m] = jnp.dot(wide[...], down_v[0], preferred_element_type=jnp.float32)
+            for k in range(1, nt):
+                at = pl.ds(pl.multiple_of(peers[k - 1] * rows, rows), rows)
+                psend[m, k - 1] = pall[m, at, :].astype(jnp.bfloat16)
+                part(m, k).start()
+        for m in range(micro):
+            x_local[m].wait()
+            mixed = pall[m, my_rows, :]
+            for k in range(1, nt):
+                part(m, k).wait_recv()
+                mixed = mixed + precv[m, k - 1].astype(jnp.float32)
+            ybuf[m] = (xin[m].astype(jnp.float32) + mixed).astype(jnp.bfloat16)
+
+            @pl.when(sec < ns - 1)
+            def _():
+                hop(0, m).start()
+
+            give(0, m)
+        trade()
+        weights_here(False)
+        for m in range(micro):
+            front(m)
+            for k in range(1, nt):
+                part(m, k).wait_send()
+
+    @pl.when(sec > 0)
+    def _():
+        weights_here(True)
+
+    @pl.when(sec >= 2)
+    def _():
+        turn()
+
+    @pl.when(final)
+    def _():
+        events(0, 1)
+
+    @pl.when(sec > 0)
+    def _():
+        for m in range(micro):
+            hop(0, m).wait_recv()
+            front(m)
+            mixed = None
+            for k in range(nt):
+                term = jnp.dot(act[k], down_v[k], preferred_element_type=jnp.float32)
+                mixed = term if mixed is None else mixed + term
+            ybuf[m] = (xin[m].astype(jnp.float32) + mixed).astype(jnp.bfloat16)
+
+            @pl.when(sec < ns - 1)
+            def _():
+                hop(0, m).start()
+
+            give(0, m)
+
+    @pl.when(sec < 2)
+    def _():
+        turn()
+
+    @pl.when(sec < ns - 1)
+    def _():
+        events(0, count)
 
     for m in range(micro):
         @pl.when(final)
@@ -289,11 +381,11 @@
         g = gin[m]
         for k in range(nt):
             for cut in cuts:
-                ga = lax.dot_general(g, down_v[k, cut, :], NT, preferred_element_type=jnp.float32)
+                ga = jnp.dot(g, down_t[k, :, cut], preferred_element_type=jnp.float32)
                 act[k, :, cut] = (ga * slope[m, k, :, cut]).astype(jnp.bfloat16)
         gn = None
         for k in range(nt):
-            term = lax.dot_general(act[k], up_v[k], NT, preferred_element_type=jnp.float32)
+            term = jnp.dot(act[k], up_t[k], preferred_element_type=jnp.float32)
             gn = term if gn is None else gn + term
         standard = xhat[m]
         dn = gn * gain
@@ -309,15 +401,9 @@
 
         give(1, m)
 
-    @pl.when(sec >= ns - 2)
-    def _():
-        for slot in range(early, middle):
-            for stream in streams:
-                stream.event(slot)
-
-    for slot in range(middle, count):
-        for stream in streams:
-            stream.event(slot)
+    @pl.when(final)
+    def _():
+        events(1, count)
 
     for stream in streams:
         stream.finish()
@@ -354,10 +440,11 @@
     bf, f32 = jnp.bfloat16, jnp.float32
     vm, dma = pltpu.VMEM, pltpu.SemaphoreType.DMA
     k = max(nt - 1, 1)
-    anywhere = pl.BlockSpec(memory_space=pl.ANY)
     inside = pl.BlockSpec(memory_space=pltpu.VMEM)
     macs = micro * rows * d * hid * nt * 4
-    outs, grads, total_up, total_down = pl.pallas_call(
+    anywhere = pl.BlockSpec(memory_space=pl.ANY)
+    hbm = pl.BlockSpec(memory_space=pltpu.HBM)
+    outs, grads, new_up, new_down = pl.pallas_call(
         functools.partial(window_kernel, ns, n, nt, chunk),
         out_shape=(
             jax.ShapeDtypeStruct((micro, tokens, d), bf),
@@ -365,16 +452,26 @@
             jax.ShapeDtypeStruct((d // n, hid), f32),
             jax.ShapeDtypeStruct((hid // n, d), f32),
         ),
-        in_specs=[anywhere, anywhere, inside] + [anywhere] * 4,
+        in_specs=[hbm] * 9,
         out_specs=(anywhere, anywhere, inside, inside),
         scratch_shapes=[
+            vm((1, d), f32),
             vm((nt, d, hid), bf),
             vm((nt, hid, d), bf),
+            vm((nt, hid, d), bf),
+            vm((nt, d, hid), bf),
+            vm((d // n, hid), f32),
+            vm((hid // n, d), f32),
+            vm((micro, tokens, d), bf),
+            vm((micro, tokens, d), f32),
+            vm((micro, k, rows, d), bf),
+            vm((micro, k, rows, d), bf),
             vm((micro, rows, d), bf),
             vm((micro, rows, d), bf),
             vm((micro, rows, d), bf),
             vm((micro, rows, d), bf),
             vm((nt, rows, hid), bf),
+            vm((tokens, hid), bf),
             vm((micro, nt, rows, hid), f32),
             vm((micro, rows, d), f32),
             vm((micro, rows, 128), f32),
@@ -382,19 +479,17 @@
             vm((n // 2, hid // n, d), bf),
             vm((n - 1, d // n, hid), bf),
             vm((n - 1, hid // n, d), bf),
-            dma((2,)), dma((2, k)), dma((2, k)),
-            dma((2, micro)), dma((2, micro)), dma((2, micro)),
+            dma((2,)), dma((3,)), dma((micro, k)), dma((micro, k)), dma((2, k)), dma((2, k)),
+            dma((3, micro)), dma((2, micro)), dma((2, micro)),
             dma((2, micro)), dma((2, micro, k)), dma((2, micro, k)),
             dma((2, n // 2)), dma((2, n - 1)), dma((2, n - 1)),
         ],
         compiler_params=pltpu.CompilerParams(
-            collective_id=0, has_side_effects=True, vmem_limit_bytes=48 * 1024 * 1024
+            collective_id=0, has_side_effects=True, vmem_limit_bytes=46 * 1024 * 1024
         ),
         cost_estimate=pl.CostEstimate(flops=2 * macs, bytes_accessed=4 * hid * d * 4, transcendentals=micro * rows * hid * nt),
         name="window",
-    )(inputs, out_grads, norm_gain, up_weight[0], down_weight[0], pu, pd)
-    new_up = master_up[0] - learning_rate * total_up
-    new_down = master_down[0] - learning_rate * total_down
+    )(inputs, out_grads, norm_gain, up_weight[0], down_weight[0], pu, pd, master_up[0], master_down[0])
     return (outs[None], grads[None], new_up[None], new_down[None])
 
 

time: 72.9 us -> 72.3 us (level)
  local copies, waits for them, and re-layouts: 4.69 us -> 8.73 us
  other arithmetic: 2.45 us -> 0 us
  Pallas kernels: 64.8 us -> 62.7 us
    unnamed x12 -> x14, local copies, waits for them, and re-layouts: 4.69 us -> 8.73 us
    broadcast_in_dim x2 -> x0, other arithmetic: 2.45 us -> none  [local(): return (outs[None], grads[None], new_up[None], new_down[None])]
    pallas_call x1, Pallas kernels: 64.8 us -> 62.7 us  [local(): pl.pallas_call(functools.partial(window_kernel, ns, n, nt, chunk), out_sh...]
where the time goes in v2:
time: 72.3 us; the launch traced here: 72 us
  Pallas kernels  62.7 us (87%)
  local copies, waits for them, and re-layouts  8.73 us (12%)
    pallas_call x1, Pallas kernels, local(): pl.pallas_call(functools.partial(window_kernel, ns, n, nt, chunk), out_sh...  62.7 us
    unnamed x14, local copies, waits for them, and re-layouts  8.73 us

profile of v2, /device:TPU:0, one launch (start us, length us, event | category | flops | bytes accessed | tf_op | source)
XLA Modules:
  0.0 72.0 jit_solution(15644168261841173347)
XLA Ops:
  0.6 0.0 copy-start
  0.6 1.3 %copy-done = f32[1,192,1536]{2,1,0:T(8,128)S(1)} copy-done((f32[1,192,1536]{2,1,0:T(8,128)S(1)}, f32[1,192,1536]{2,1,0:T(8,128)}, u32[]{:S(2)}) %copy-start) | copy-done | bytes 1179672
  1.9 0.0 copy-start.1
  1.9 1.3 %copy-done.1 = f32[1,384,768]{2,1,0:T(8,128)S(1)} copy-done((f32[1,384,768]{2,1,0:T(8,128)S(1)}, f32[1,384,768]{2,1,0:T(8,128)}, u32[]{:S(2)}) %copy-start.1) | copy-done | bytes 1179672
  3.2 0.0 copy-start.2
  3.2 1.0 %copy-done.2 = bf16[2,128,768]{2,1,0:T(8,128)(2,1)S(1)} copy-done((bf16[2,128,768]{2,1,0:T(8,128)(2,1)S(1)}, bf16[2,128,768]{2,1,0:T(8,128)(2,1)}, u32[]{:S(2)}) %copy-start.2) | copy-done | bytes 393240
  4.2 0.0 copy-start.3
  4.2 1.0 %copy-done.3 = bf16[2,128,768]{2,1,0:T(8,128)(2,1)S(1)} copy-done((bf16[2,128,768]{2,1,0:T(8,128)(2,1)S(1)}, bf16[2,128,768]{2,1,0:T(8,128)(2,1)}, u32[]{:S(2)}) %copy-start.3) | copy-done | bytes 393240
  5.2 0.0 copy-start.4
  5.2 0.7 copy-done.4
  5.9 62.7 %window.1 = (bf16[2,128,768]{2,1,0:T(8,128)(2,1)S(1)}, bf16[2,128,768]{2,1,0:T(8,128)(2,1)S(1)}, f32[192,1536]{1,0:T(8,128)S(1)}, f32[384,768]{1,0:T(8,128)S(1)}) custom-call(bf16[2,128,768]{2,1,0:T(8,128)(2,1)S(1)} %copy-done.2, bf16[2,128,768]{2,1,0:T(8,128)(2,1)S(1)} %copy-done.3, f32[1,768]{1,0:T(1,128)S(1)} %copy-done.4, bf16[768,1536]{1,0:T(8,128)(2,1)} %bitcast.16, ...), custom_call_target="tpu_custom_call" | custom-call | flops 2415919104 | bytes 18874368 | tf_op jit(solution)/shard_map/window/pallas_call | solution.py:447
  68.5 0.7 %copy.17 = bf16[1,2,128,768]{3,2,1,0:T(8,128)(2,1)} copy(bf16[1,2,128,768]{3,2,1,0:T(8,128)(2,1)S(1)} %bitcast.15) | data formatting | bytes 786432
  69.3 0.7 %copy.18 = bf16[1,2,128,768]{3,2,1,0:T(8,128)(2,1)} copy(bf16[1,2,128,768]{3,2,1,0:T(8,128)(2,1)S(1)} %bitcast.14) | data formatting | bytes 786432
  70.0 1.0 %copy.19 = f32[1,192,1536]{2,1,0:T(8,128)} copy(f32[1,192,1536]{2,1,0:T(8,128)S(1)} %bitcast.11) | data formatting | bytes 2359296
  71.0 1.0 %copy.20 = f32[1,384,768]{2,1,0:T(8,128)} copy(f32[1,384,768]{2,1,0:T(8,128)S(1)} %bitcast.10) | data formatting | bytes 2359296
Async XLA Ops:
  0.6 1.3 %copy-start = (f32[1,192,1536]{2,1,0:T(8,128)S(1)}, f32[1,192,1536]{2,1,0:T(8,128)}, u32[]{:S(2)}) copy-start(f32[1,192,1536]{2,1,0:T(8,128)} %param.16) | copy-start | bytes 3538948
  1.9 1.3 %copy-start.1 = (f32[1,384,768]{2,1,0:T(8,128)S(1)}, f32[1,384,768]{2,1,0:T(8,128)}, u32[]{:S(2)}) copy-start(f32[1,384,768]{2,1,0:T(8,128)} %param.17) | copy-start | bytes 3538948
  3.2 1.0 %copy-start.2 = (bf16[2,128,768]{2,1,0:T(8,128)(2,1)S(1)}, bf16[2,128,768]{2,1,0:T(8,128)(2,1)}, u32[]{:S(2)}) copy-start(bf16[2,128,768]{2,1,0:T(8,128)(2,1)} %x_hbm.1) | copy-start | bytes 1179652
  4.2 1.0 %copy-start.3 = (bf16[2,128,768]{2,1,0:T(8,128)(2,1)S(1)}, bf16[2,128,768]{2,1,0:T(8,128)(2,1)}, u32[]{:S(2)}) copy-start(bf16[2,128,768]{2,1,0:T(8,128)(2,1)} %g_hbm.1) | copy-start | bytes 1179652
  5.2 0.7 copy-start.4

commit v3 on v2

--- a/solution.py
+++ b/solution.py
@@ -69,6 +69,8 @@
         for slot, (p, _) in enumerate(self.slots):
             if p == 0:
                 self.copy(slot).start()
+
+    def begin_loads(self):
         for k in range(len(self.kept)):
             self.load(k).start()
 
@@ -198,8 +200,17 @@
     )
     for stream in streams:
         stream.begin()
-    for c in own_m:
-        c.start()
+
+    def loads():
+        for stream in streams:
+            stream.begin_loads()
+        for c in own_m:
+            c.start()
+
+    @pl.when(sec > 0)
+    def _():
+        loads()
+
 
     def hop(back, m):
         return pltpu.make_async_remote_copy(
@@ -326,6 +337,7 @@
 
             give(0, m)
         trade()
+        loads()
         weights_here(False)
         for m in range(micro):
             front(m)
@@ -447,10 +459,10 @@
     outs, grads, new_up, new_down = pl.pallas_call(
         functools.partial(window_kernel, ns, n, nt, chunk),
         out_shape=(
-            jax.ShapeDtypeStruct((micro, tokens, d), bf),
-            jax.ShapeDtypeStruct((micro, tokens, d), bf),
-            jax.ShapeDtypeStruct((d // n, hid), f32),
-            jax.ShapeDtypeStruct((hid // n, d), f32),
+            pltpu.VMEM((micro, tokens, d), bf),
+            pltpu.VMEM((micro, tokens, d), bf),
+            pltpu.VMEM((d // n, hid), f32),
+            pltpu.VMEM((hid // n, d), f32),
         ),
         in_specs=[hbm] * 9,
         out_specs=(anywhere, anywhere, inside, inside),
@@ -485,7 +497,7 @@
             dma((2, n // 2)), dma((2, n - 1)), dma((2, n - 1)),
         ],
         compiler_params=pltpu.CompilerParams(
-            collective_id=0, has_side_effects=True, vmem_limit_bytes=46 * 1024 * 1024
+            collective_id=0, has_side_effects=True, vmem_limit_bytes=54 * 1024 * 1024
         ),
         cost_estimate=pl.CostEstimate(flops=2 * macs, bytes_accessed=4 * hid * d * 4, transcendentals=micro * rows * hid * nt),
         name="window",

time: 72.3 us -> 67 us (0.927)
  local copies, waits for them, and re-layouts: 8.73 us -> 3.52 us
    unnamed x14 -> x4, local copies, waits for them, and re-layouts: 8.73 us -> 3.52 us
where the time goes in v3:
time: 67 us; the launch traced here: 66.9 us
  Pallas kernels  62.7 us (94%)
  local copies, waits for them, and re-layouts  3.52 us (5%)
    pallas_call x1, Pallas kernels, local(): pl.pallas_call(functools.partial(window_kernel, ns, n, nt, chunk), out_sh...  62.7 us
    unnamed x4, local copies, waits for them, and re-layouts  3.52 us

profile of v3, /device:TPU:0, one launch (start us, length us, event | category | flops | bytes accessed | tf_op | source)
XLA Modules:
  0.0 66.9 jit_solution(13481894746595022065)
XLA Ops:
  0.6 62.7 %window.1 = (bf16[2,128,768]{2,1,0:T(8,128)(2,1)S(1)}, bf16[2,128,768]{2,1,0:T(8,128)(2,1)S(1)}, f32[192,1536]{1,0:T(8,128)S(1)}, f32[384,768]{1,0:T(8,128)S(1)}) custom-call(bf16[2,128,768]{2,1,0:T(8,128)(2,1)} %x_hbm.1, bf16[2,128,768]{2,1,0:T(8,128)(2,1)} %g_hbm.1, f32[1,768]{1,0:T(1,128)} %gain_hbm.1, bf16[768,1536]{1,0:T(8,128)(2,1)} %bitcast.14, ...), custom_call_target="tpu_custom_call" | custom-call | flops 2415919104 | bytes 18874368 | tf_op jit(solution)/shard_map/window/pallas_call | solution.py:459
  63.3 0.7 %copy.17 = bf16[1,2,128,768]{3,2,1,0:T(8,128)(2,1)} copy(bf16[1,2,128,768]{3,2,1,0:T(8,128)(2,1)S(1)} %bitcast.13) | data formatting | bytes 786432
  64.1 0.7 %copy.18 = bf16[1,2,128,768]{3,2,1,0:T(8,128)(2,1)} copy(bf16[1,2,128,768]{3,2,1,0:T(8,128)(2,1)S(1)} %bitcast.12) | data formatting | bytes 786432
  64.8 1.0 %copy.19 = f32[1,192,1536]{2,1,0:T(8,128)} copy(f32[1,192,1536]{2,1,0:T(8,128)S(1)} %bitcast.11) | data formatting | bytes 2359296
  65.8 1.0 %copy.20 = f32[1,384,768]{2,1,0:T(8,128)} copy(f32[1,384,768]{2,1,0:T(8,128)S(1)} %bitcast.10) | data formatting | bytes 2359296
